TPU v7x, 32 devices: a whole 2x2x4 slice. The times are simulated.
32 devices in a mesh: wide: 4 (over x, core), col: 8 (over z, y).
Axes of the slice: x: 2, y: 2, z: 4, core: 2. Of those that a mesh axis runs over, the one named last changes fastest.
Arguments:
- adjoint: bfloat16 [32, 1536], P(None, ('wide', 'col')), may hold values from -6 to 6
- operator: bfloat16 [1536, 196608], P('wide', 'col'), may hold values from -0.21875 to 0.21875
- owner: int32 [196608], P(('col', 'wide')), may hold values from 0 to 196607, as said below
Outputs:
- junction_sums: float32 [32, 196608], P(None, ('col', 'wide'))
Inputs may be any that keep to these rules, and one draw needn't show every extreme that they name: Unknown j of device block b = j // 6144 (blocks ordered col first, then wide) has owner j itself, or is a duplicate whose owner is an unknown in the lower half of a block of the same index of col; duplicates lie only in the upper half of a block and owners of duplicates are never duplicates. One block hands at most 16 duplicates to the blocks of any one index of wide, and this count is reached in every draw, by some block towards every index of wide and towards some index of wide from every block.
All inputs are finite; a program needn't handle non-finite values.
Results may differ from a plain program's by a relative error of at most 0.0003.
Values may be sent and summed in bfloat16 or wider, within the bound.
A program may use at most 64 MiB of HBM per device.

v0:
```python
import jax
import jax.numpy as jnp
from jax import lax
from jax.sharding import PartitionSpec as P

CAP = 16


def local(adjoint, operator, owner):
    wide_count = lax.axis_size("wide")
    own_width = owner.shape[0]
    block_cols = operator.shape[1]
    sensors = adjoint.shape[0]
    partials = jnp.dot(
        lax.all_gather(adjoint, "col", axis=1, tiled=True),
        operator,
        preferred_element_type=jnp.float32,
    )
    col_base = lax.axis_index("col") * block_cols
    summed = lax.psum_scatter(partials, "wide", scatter_dimension=1, tiled=True)
    positions = jnp.arange(own_width, dtype=jnp.int32)
    global_cols = col_base + lax.axis_index("wide") * own_width + positions
    repeated = owner != global_cols
    target_peer = owner // own_width % wide_count
    target_place = owner % own_width
    peers = jnp.arange(wide_count, dtype=jnp.int32)
    marks = ((target_peer[:, None] == peers[None, :]) & repeated[:, None]).astype(jnp.int32)
    ranking = jnp.sum((jnp.cumsum(marks, axis=0) - marks) * marks, axis=1)
    slot_of = target_peer * CAP + ranking
    slot_ids = jnp.arange(wide_count * CAP, dtype=jnp.int32)
    chosen = (slot_of[:, None] == slot_ids[None, :]) & repeated[:, None]
    selector = chosen.astype(jnp.float32)
    outgoing = jnp.dot(
        summed, selector, precision=lax.Precision.HIGHEST, preferred_element_type=jnp.float32
    )
    place_sum = jnp.sum(chosen.astype(jnp.int32) * (target_place + 1)[:, None], axis=0) - 1
    outgoing = outgoing.reshape(sensors, wide_count, CAP)
    places = place_sum.astype(jnp.float32).reshape(1, wide_count, CAP)
    arrived, arrived_places = (
        lax.all_to_all(outgoing, "wide", split_axis=1, concat_axis=1, tiled=True),
        lax.all_to_all(places, "wide", split_axis=1, concat_axis=1, tiled=True),
    )
    flat_values = arrived.reshape(sensors, wide_count * CAP)
    landing = arrived_places.reshape(-1).astype(jnp.int32)
    receiver = (landing[:, None] == positions[None, :]).astype(jnp.float32)
    kept = summed * (1.0 - repeated.astype(jnp.float32))[None, :]
    added = jnp.dot(
        flat_values, receiver, precision=lax.Precision.HIGHEST, preferred_element_type=jnp.float32
    )
    return kept + added


def solution(mesh):
    return jax.shard_map(
        local,
        mesh=mesh,
        in_specs=(P(None, ("wide", "col")), P("wide", "col"), P(("col", "wide"))),
        out_specs=P(None, ("col", "wide")),
        check_vma=False,
    )
```

profile of v0, /device:TPU:0, one launch (start us, length us, event | category | flops | bytes accessed | tf_op | source)
XLA Modules:
  0.0 109.2 jit_solution(1347865884361910473)
XLA Ops:
  6.5 0.0 reduce-scatter.2.cloned.1.call-start
  6.5 32.5 %all-gather = bf16[8,48,32]{1,2,0:T(8,128)(2,1)S(1)} all-gather(bf16[1,48,32]{1,2,0:T(8,128)(2,1)} %bitcast.40), channel_id=1, replica_groups=mesh['wide'=4,'col'=8] {'col'}, dimensions={0}, use_global_device_ids=true | all-gather | bytes 27648 | tf_op jit(solution)/shard_map/all_gather | solution.py:15
  39.1 0.1 reshape.58
  39.2 11.4 %fusion.15 = f32[32,24576]{1,0:T(8,128)} fusion(bf16[384,32]{0,1:T(8,128)(2,1)S(1)} %reshape.58, bf16[384,24576]{1,0:T(8,128)(2,1)} %param.4), kind=kOutput, calls=%fused_computation.35 | convolution fusion | flops 603979776 | bytes 22044672 | tf_op jit(solution)/shard_map/dot_general | solution.py:14
  50.6 0.0 copy-start.1
  50.6 0.0 reduce-scatter.2.cloned.1.call-update
  50.6 0.7 copy-done.1
  51.4 1.2 %reduce-window.6 = s32[4,48,128]{2,1,0:T(8,128)S(1)} reduce-window(s32[4,48,128]{2,1,0:T(8,128)S(1)} %fusion.11, s32[]{:T(128)} %constant.49.clone.1), window={size=1x1x128 pad=0_0x0_0x127_0}, to_apply=%region_1.2 | reduce-window | flops 3121152 | bytes 196612 | tf_op jit(solution)/shard_map/reduce-window
  52.6 0.2 slice_reduce_fusion
  52.8 0.2 reduce-window.9
  53.0 0.1 add_bitcast_fusion
  53.1 0.1 fusion.8
  53.3 0.4 select_reduce_fusion
  53.7 0.7 convert_element_type.40
  54.3 3.2 %all-to-all-start.1 = ((f32[1,4,16]{2,0,1:T(1,128)}), f32[1,4,16]{2,0,1:T(1,128)S(1)}, u32[]{:S(2)}, u32[]{:S(2)}) async-start(f32[1,4,16]{2,0,1:T(1,128)} %bitcast.7), calls=%async_computation.2 | async-start | bytes 4096 | tf_op jit(solution)/shard_map/all_to_all | solution.py:41
  57.5 32.0 %reduce-scatter.2.cloned.1.call-done = f32[32,6144]{1,0:T(8,128)} async-done(((f32[32,24576]{1,0:T(8,128)}), f32[32,6144]{1,0:T(8,128)}) %reduce-scatter.2.cloned.1.call-update) | async-done | bytes 786448 | tf_op jit(solution)/shard_map/reduce_scatter | solution.py:20
  89.6 0.0 copy-start
  89.6 2.2 %fusion.1 = f32[32,64]{0,1:T(8,128)S(1)} fusion(f32[32,6144]{1,0:T(8,128)} %reduce-scatter.2.cloned.1.call-done, s32[6144]{0:T(1024)S(1)} %multiply_add_fusion, pred[6144]{0:T(1024)(128)(4,1)S(1)} %get-tuple-element.6), kind=kOutput, calls=%fused_computation.5 | convolution fusion | flops 151781376 | bytes 825344 | tf_op jit(solution)/shard_map/dot_general | solution.py:33
  91.8 0.7 reshape.67
  92.5 0.0 all-to-all-done.1
  92.5 3.2 %all-to-all-start = ((f32[4,1,512]{2,1,0:T(1,128)}), f32[4,1,512]{2,1,0:T(1,128)S(1)}, u32[]{:S(2)}, u32[]{:S(2)}) async-start(f32[4,1,512]{2,1,0:T(1,128)} %reshape.67), calls=%async_computation.1 | async-start | bytes 16384 | tf_op jit(solution)/shard_map/all_to_all | solution.py:40
  95.8 0.1 convert_element_type.42
  95.8 3.7 %all-to-all-done = f32[4,1,512]{2,1,0:T(1,128)S(1)} async-done(((f32[4,1,512]{2,1,0:T(1,128)}), f32[4,1,512]{2,1,0:T(1,128)S(1)}, u32[]{:S(2)}, u32[]{:S(2)}) %all-to-all-start) | async-done | bytes 8224 | tf_op jit(solution)/shard_map/all_to_all | solution.py:40
  99.5 0.5 broadcast.59
  100.0 0.7 reduce.6
  100.7 0.1 reshape.68
  100.8 0.0 copy-done
  100.8 1.6 %convolution_add_fusion = f32[32,6144]{1,0:T(8,128)} fusion(f32[32,64]{0,1:T(8,128)S(1)} %bitcast.36, s32[64]{0:T(128)S(1)} %convert_element_type.42, f32[32,6144]{1,0:T(8,128)S(1)} %copy-done, f32[6144]{0:T(1024)S(1)} %get-tuple-element.5), kind=kOutput, calls=%fused_computation | convolution fusion | flops 151781376 | bytes 1605888 | tf_op jit(solution)/shard_map/dot_general | solution.py:47
  (7 shorter events, 0.1 us)
Async XLA Ops:
  6.5 83.1 %reduce-scatter.2.cloned.1.call-start = ((), (), s32[]{:S(2)}) async-start(), calls=%async_computation.3 | async-start | bytes 3932160 | tf_op jit(solution)/shard_map/reduce_scatter | solution.py:20
  50.6 0.7 copy-start.1
  54.3 38.1 %all-to-all-start.1 = ((f32[1,4,16]{2,0,1:T(1,128)}), f32[1,4,16]{2,0,1:T(1,128)S(1)}, u32[]{:S(2)}, u32[]{:S(2)}) async-start(f32[1,4,16]{2,0,1:T(1,128)} %bitcast.7), calls=%async_computation.2 | async-start | bytes 4096 | tf_op jit(solution)/shard_map/all_to_all | solution.py:41
  89.6 11.2 %copy-start = (f32[32,6144]{1,0:T(8,128)S(1)}, f32[32,6144]{1,0:T(8,128)}, u32[]{:S(2)}) copy-start(f32[32,6144]{1,0:T(8,128)} %reduce-scatter.2.cloned.1.call-done) | copy-start | bytes 2359300
  92.5 7.0 %all-to-all-start = ((f32[4,1,512]{2,1,0:T(1,128)}), f32[4,1,512]{2,1,0:T(1,128)S(1)}, u32[]{:S(2)}, u32[]{:S(2)}) async-start(f32[4,1,512]{2,1,0:T(1,128)} %reshape.67), calls=%async_computation.1 | async-start | bytes 16384 | tf_op jit(solution)/shard_map/all_to_all | solution.py:40
Sparse Core Ops, SparseCore 0:
  50.7 38.8 reduce-scatter.1
where the time goes:
time: 110 us; the launch traced here: 109 us
  waiting for transfers between devices  35.7 us (32%)
  blocking collectives  32.5 us (30%)
  matrix products  15.2 us (14%)
  between operations  13.5 us (12%)
  starting transfers between devices  6.44 us (6%)
  local copies, waits for them, and re-layouts  3.09 us (3%)
  other arithmetic  2.82 us (3%)
    all_gather x1, blocking collectives, local(): lax.all_gather(adjoint, 'col', axis=1, tiled=True)  32.5 us
    reduce_scatter x1, waiting for transfers between devices, local(): summed = lax.psum_scatter(partials, 'wide', scatter_dimension=1, tiled=True)  32 us
    dot_general x1, matrix products, local(): jnp.dot(lax.all_gather(adjoint, 'col', axis=1, tiled=True), operator, pre...  11.4 us
    all_to_all x1, waiting for transfers between devices, local(): lax.all_to_all(outgoing, 'wide', split_axis=1, concat_axis=1, tiled=True)  3.67 us
    all_to_all x1, starting transfers between devices, local(): lax.all_to_all(outgoing, 'wide', split_axis=1, concat_axis=1, tiled=True)  3.25 us
    all_to_all x1, starting transfers between devices, local(): lax.all_to_all(places, 'wide', split_axis=1, concat_axis=1, tiled=True)  3.19 us
  transfers between devices with their start and end apart: 3, of which 2 were waited for; matrix products, arithmetic and copies ran while one was open for 5% of the time, Pallas kernels for 0%

commit v1 on v0

v1 whole, which is shorter than its diff:
```python
import functools

import jax
import jax.numpy as jnp
from jax import lax
from jax.experimental import pallas as pl
from jax.experimental.pallas import tpu as pltpu
from jax.sharding import PartitionSpec as P

CAP = 16
LANES = 128
MESH = pl.DeviceIdType.MESH
F32 = jnp.float32
BF16 = jnp.bfloat16


def split(x):
    high = x.astype(BF16)
    low = (x - high.astype(F32)).astype(BF16)
    return jnp.concatenate([high, low], axis=0)


def kernel(
    wide_count, col_count, chunks,
    adj_ref, op_ref, own_ref, out_ref,
    op_buf, adj_buf, a_buf, owners, sib_out, sib_in, mine, far_in, hot, place_buf, dup_out, dup_in,
    op_sem, adj_send, adj_recv, own_send, own_recv, sib_send, sib_recv, far_send, far_recv, dup_send, dup_recv,
):
    chips = wide_count // 2
    sensors, depth = adj_ref.shape
    rows, width, chunk = op_buf.shape[1], out_ref.shape[1], op_buf.shape[2]
    half = width // 2
    half_rows = half // LANES
    slots = wide_count * CAP
    all_slots = chips * slots
    w, k = lax.axis_index("wide"), lax.axis_index("col")
    g, c = w // 2, lax.rem(w, 2)

    def ahead(e, other):
        return lax.rem(g + e, chips) * 2 + (1 - c if other else c)

    steps = [(e, q) for e in list(range(1, chips)) + [0] for q in range(chunks)]
    loads = []
    for n, (e, q) in enumerate(steps):
        for other in (1, 0):
            start = pl.multiple_of(ahead(e, other) * width + q * chunk, LANES)
            i = 2 * n + 1 - other
            load = pltpu.make_async_copy(op_ref.at[:, pl.ds(start, chunk)], op_buf.at[i], op_sem.at[i])
            load.start()
            loads.append(load)

    adj_buf[k] = jnp.zeros(adj_buf.shape[1:], BF16)
    adj_buf[k, :, :depth] = adj_ref[...]
    pairs = [(e, other) for e in range(chips) for other in (0, 1)][1:]

    barrier = pltpu.get_barrier_semaphore()
    for d in range(1, col_count):
        pl.semaphore_signal(barrier, inc=1, device_id={"col": lax.rem(k + d, col_count)}, device_id_type=MESH)
    for e, other in pairs:
        pl.semaphore_signal(barrier, inc=1, device_id={"wide": ahead(e, other)}, device_id_type=MESH)
    pl.semaphore_wait(barrier, col_count - 1 + wide_count - 1)

    adj_copies = []
    for d in range(1, col_count):
        copy = pltpu.make_async_remote_copy(
            adj_buf.at[k], adj_buf.at[k], adj_send.at[d - 1], adj_recv.at[d - 1],
            device_id={"col": lax.rem(k + d, col_count)}, device_id_type=MESH)
        copy.start()
        adj_copies.append(copy)
    own_copies = []
    for e, other in pairs:
        at = 2 * e + other
        copy = pltpu.make_async_remote_copy(
            own_ref, owners.at[at], own_send.at[at], own_recv.at[at],
            device_id={"wide": ahead(e, other)}, device_id_type=MESH)
        copy.start()
        own_copies.append(copy)

    for d in range(1, col_count):
        source = lax.rem(k - d + col_count, col_count)
        pltpu.make_async_remote_copy(
            adj_buf.at[source], adj_buf.at[source], adj_send.at[d - 1], adj_recv.at[d - 1],
            device_id={"col": source}, device_id_type=MESH).wait_recv()
    padded = adj_buf.shape[2]
    total = jnp.zeros((sensors, rows), F32)
    from_row = lax.broadcasted_iota(jnp.int32, (padded, rows), 0)
    to_row = lax.broadcasted_iota(jnp.int32, (padded, rows), 1)
    for i in range(col_count):
        shift = (from_row < depth) & (to_row == from_row + i * depth)
        total += jnp.dot(adj_buf[i], shift.astype(F32).astype(BF16), preferred_element_type=F32)
    a_buf[...] = total.astype(BF16)

    def product(i):
        loads[i].wait()
        return jnp.dot(a_buf[...], op_buf[i], preferred_element_type=F32)

    sent = []

    def combine(e, q):
        sib_copies[(e, q)].wait_recv()
        mine[e, q] += sib_in[e, q]
        if e > 0:
            copy = pltpu.make_async_remote_copy(
                mine.at[e, q], far_in.at[e - 1, q], far_send.at[e - 1, q], far_recv.at[e - 1, q],
                device_id={"wide": ahead(e, 0)}, device_id_type=MESH)
            copy.start()
            sent.append((e, q, copy))

    sib_copies = {}
    for n, (e, q) in enumerate(steps):
        sib_out[e, q] = product(2 * n)
        copy = pltpu.make_async_remote_copy(
            sib_out.at[e, q], sib_in.at[e, q], sib_send.at[e, q], sib_recv.at[e, q],
            device_id={"wide": ahead(0, 1)}, device_id_type=MESH)
        copy.start()
        sib_copies[(e, q)] = copy
        mine[e, q] = product(2 * n + 1)
        if n > 0:
            combine(*steps[n - 1])
    combine(*steps[-1])

    for copy in own_copies:
        copy.wait_recv()
    lane_in = lax.broadcasted_iota(jnp.int32, (LANES, LANES), 0)
    lane_out = lax.broadcasted_iota(jnp.int32, (LANES, LANES), 1)
    before = (lane_in < lane_out).astype(F32).astype(BF16)
    ones = jnp.ones((LANES, LANES), BF16)
    slot_ids = lax.broadcasted_iota(jnp.int32, (all_slots, LANES), 0).astype(F32)
    columns = (lax.broadcasted_iota(jnp.int32, (half_rows, LANES), 0) * LANES
               + lax.broadcasted_iota(jnp.int32, (half_rows, LANES), 1))

    def marks(owner, block):
        return owner != k * (width * wide_count) + block * width + half + columns

    for other in (0, 1):
        place = jnp.zeros((all_slots, LANES), F32)
        for e in range(chips):
            chip = lax.rem(g - e + chips, chips)
            block = chip * 2 + (1 - c if other else c)
            owner = own_ref[half_rows:, :] if (e, other) == (0, 0) else owners[2 * e + other, half_rows:, :]
            repeated = marks(owner, block)
            flags = repeated.astype(F32).astype(BF16)
            ranks = jnp.dot(flags, before, preferred_element_type=F32)
            counts = jnp.dot(flags, ones, preferred_element_type=F32)
            target = (owner - k * (width * wide_count) + 1).astype(F32)
            base = jnp.zeros((1, LANES), F32) + (chip * slots).astype(F32)
            for r in range(half_rows):
                slot = jnp.where(repeated[r : r + 1, :], ranks[r : r + 1, :] + base, -1.0)
                base = base + counts[r : r + 1, :]
                chosen = slot_ids == slot
                place = place + jnp.where(chosen, target[r : r + 1, :], 0.0)
                if other == 0:
                    hot[chip, :, r * LANES : (r + 1) * LANES] = chosen.astype(F32).astype(BF16)
        place_buf[other] = jnp.sum(place, axis=1, keepdims=True) - 1.0

    nt = (((1,), (1,)), ((), ()))
    picked = jnp.zeros((2 * sensors, all_slots), F32)
    for e in range(chips):
        for q in range(chunks // 2, chunks):
            start = (q - chunks // 2) * chunk
            picked += lax.dot_general(
                split(mine[e, q]), hot[lax.rem(g + e, chips), :, start : start + chunk], nt,
                preferred_element_type=F32)
    dup_out[...] = picked[:sensors] + picked[sensors:]
    dup_copies = []
    for e, other in pairs:
        at = 2 * e + other
        copy = pltpu.make_async_remote_copy(
            dup_out, dup_in.at[at], dup_send.at[at], dup_recv.at[at],
            device_id={"wide": ahead(e, other)}, device_id_type=MESH)
        copy.start()
        dup_copies.append(copy)
    repeated = marks(own_ref[half_rows:, :], w)
    kept = 1.0 - repeated.astype(F32)
    for copy in dup_copies:
        copy.wait_recv()
    sums = [dup_out[...], None]
    for e, other in pairs:
        value = dup_in[2 * e + other]
        sums[other] = value if sums[other] is None else sums[other] + value
    sums = [split(value) for value in sums]
    for q in range(chunks // 2):
        mine_at = (lax.broadcasted_iota(jnp.int32, (all_slots, chunk), 1) + (w * width + q * chunk)).astype(F32)
        for other in (0, 1):
            lands = (mine_at == place_buf[other]).astype(F32).astype(BF16)
            added = jnp.dot(sums[other], lands, preferred_element_type=F32)
            mine[0, q] += added[:sensors] + added[sensors:]

    for q in range(chunks):
        value = mine[0, q]
        for e, at, copy in sent:
            if at == q:
                copy.wait_recv()
                value = value + far_in[e - 1, q]
        if q >= chunks // 2:
            first = (q - chunks // 2) * chunk // LANES
            parts = []
            for r in range(chunk // LANES):
                keep = jnp.broadcast_to(kept[first + r : first + r + 1, :], (sensors, LANES))
                parts.append(jnp.where(keep > 0.5, value[:, r * LANES : (r + 1) * LANES], 0.0))
            value = jnp.concatenate(parts, axis=1)
        out_ref[:, q * chunk : (q + 1) * chunk] = value

    for copy in adj_copies + own_copies + dup_copies + list(sib_copies.values()) + [s[2] for s in sent]:
        copy.wait_send()


def local(adjoint, operator, owner):
    wide_count, col_count = lax.axis_size("wide"), lax.axis_size("col")
    chips = wide_count // 2
    sensors, depth = adjoint.shape
    rows, block_cols = operator.shape
    width = block_cols // wide_count
    half = width // 2
    chunks = 4 if half % (2 * LANES) == 0 else 2
    chunk = width // chunks
    padded = -(-depth // LANES) * LANES
    all_slots = chips * wide_count * CAP
    pieces = (chips, chunks, sensors, chunk)
    dma = pltpu.SemaphoreType.DMA
    vmem = pl.BlockSpec(memory_space=pltpu.VMEM)
    return pl.pallas_call(
        functools.partial(kernel, wide_count, col_count, chunks),
        out_shape=jax.ShapeDtypeStruct((sensors, width), F32),
        in_specs=[vmem, pl.BlockSpec(memory_space=pl.ANY), vmem],
        out_specs=vmem,
        scratch_shapes=[
            pltpu.VMEM((wide_count * chunks, rows, chunk), BF16),
            pltpu.VMEM((col_count, sensors, padded), BF16),
            pltpu.VMEM((sensors, rows), BF16),
            pltpu.VMEM((wide_count, width // LANES, LANES), jnp.int32),
            pltpu.VMEM(pieces, F32),
            pltpu.VMEM(pieces, F32),
            pltpu.VMEM(pieces, F32),
            pltpu.VMEM((chips - 1,) + pieces[1:], F32),
            pltpu.VMEM((chips, all_slots, half), BF16),
            pltpu.VMEM((2, all_slots, 1), F32),
            pltpu.VMEM((sensors, all_slots), F32),
            pltpu.VMEM((wide_count, sensors, all_slots), F32),
            dma((wide_count * chunks,)),
            dma((col_count - 1,)), dma((col_count - 1,)),
            dma((wide_count,)), dma((wide_count,)),
            dma(pieces[:2]), dma(pieces[:2]),
            dma((chips - 1, chunks)), dma((chips - 1, chunks)),
            dma((wide_count,)), dma((wide_count,)),
        ],
        compiler_params=pltpu.CompilerParams(
            collective_id=0, has_side_effects=True, vmem_limit_bytes=56 * 1024 * 1024),
        cost_estimate=pl.CostEstimate(
            flops=2 * sensors * rows * block_cols, bytes_accessed=2 * rows * block_cols, transcendentals=0),
    )(adjoint, operator, owner.reshape(width // LANES, LANES))


def solution(mesh):
    return jax.shard_map(
        local,
        mesh=mesh,
        in_specs=(P(None, ("wide", "col")), P("wide", "col"), P(("col", "wide"))),
        out_specs=P(None, ("col", "wide")),
        check_vma=False,
    )
```

time: 110 us -> 35.6 us (0.32)
  waiting for transfers between devices: 35.7 us -> 0 us
  Pallas kernels: 0 us -> 33.3 us
  blocking collectives: 32.5 us -> 0 us
  matrix products: 15.2 us -> 0 us
  between operations: 13.5 us -> 0.01 us
  starting transfers between devices: 6.44 us -> 0 us
  other arithmetic: 2.82 us -> 0 us
    pallas_call x0 -> x1, Pallas kernels: none -> 33.3 us  [local(): pl.pallas_call(functools.partial(kernel, wide_count, col_count, chunks),...]
    all_gather x1 -> x0, blocking collectives: 32.5 us -> none  [local(): lax.all_gather(adjoint, 'col', axis=1, tiled=True)]
    reduce_scatter x1 -> x0, waiting for transfers between devices: 32 us -> none  [local(): summed = lax.psum_scatter(partials, 'wide', scatter_dimension=1, tiled=True)]
    dot_general x3 -> x0, matrix products: 15.2 us -> none  [the longest x1 11.4 us: local(): jnp.dot(lax.all_gather(adjoint, 'col', axis=1, tiled=True), operator, pre...]
    all_to_all x2 -> x0, starting transfers between devices: 6.44 us -> none  [the longest x1 3.25 us: local(): lax.all_to_all(outgoing, 'wide', split_axis=1, concat_axis=1, tiled=True)]
    all_to_all x2 -> x0, waiting for transfers between devices: 3.67 us -> none  [the longest x1 3.67 us: local(): lax.all_to_all(outgoing, 'wide', split_axis=1, concat_axis=1, tiled=True)]
    another operation x2 -> x0, other arithmetic: 1.42 us -> none
  transfers between devices with their start and end apart: 3 -> 0, of which waited for: 2 -> 0; matrix products, arithmetic and copies ran while one was open for 5% -> 0% of each run, Pallas kernels for 0% -> 0%
where the time goes in v1:
time: 35.6 us; the launch traced here: 35.4 us
  Pallas kernels  33.3 us (94%)
  local copies, waits for them, and re-layouts  2.06 us (6%)
    pallas_call x1, Pallas kernels, local(): pl.pallas_call(functools.partial(kernel, wide_count, col_count, chunks),...  33.3 us
    unnamed x1, local copies, waits for them, and re-layouts  2.06 us

profile of v1, /device:TPU:0, one launch (start us, length us, event | category | flops | bytes accessed | tf_op | source)
XLA Modules:
  0.0 35.4 jit_solution(4937672091753322535)
XLA Ops:
  0.0 33.3 %shard_map.37 = f32[32,6144]{1,0:T(8,128)} custom-call(bf16[32,48]{1,0:T(8,128)(2,1)} %adj_ref.1, bf16[384,24576]{1,0:T(8,128)(2,1)} %op_ref.1, s32[48,128]{1,0:T(8,128)} %bitcast.1), custom_call_target="tpu_custom_call" | custom-call | flops 603979776 | bytes 18874368 | tf_op jit(solution)/shard_map/pallas_call | solution.py:222
  33.3 2.1 %copy.5 = f32[32,6144]{1,0:T(8,128)} copy(f32[32,6144]{1,0:T(8,128)} %shard_map.37) | data formatting | bytes 1572864

commit v2 on v1

--- a/solution.py
+++ b/solution.py
@@ -9,6 +9,7 @@
 
 CAP = 16
 LANES = 128
+LEVELS = 32767.0
 MESH = pl.DeviceIdType.MESH
 F32 = jnp.float32
 BF16 = jnp.bfloat16
@@ -23,8 +24,8 @@
 def kernel(
     wide_count, col_count, chunks,
     adj_ref, op_ref, own_ref, out_ref,
-    op_buf, adj_buf, a_buf, owners, sib_out, sib_in, mine, far_in, hot, place_buf, dup_out, dup_in,
-    op_sem, adj_send, adj_recv, own_send, own_recv, sib_send, sib_recv, far_send, far_recv, dup_send, dup_recv,
+    op_buf, adj_buf, a_buf, owners, sib_out, sib_in, mine, far_out, far_in, top_out, top_in, hot, lands, place_buf, dup_out, dup_in,
+    op_sem, adj_send, adj_recv, own_send, own_recv, sib_send, sib_recv, far_send, far_recv, top_send, top_recv, dup_send, dup_recv,
 ):
     chips = wide_count // 2
     sensors, depth = adj_ref.shape
@@ -75,6 +76,39 @@
             device_id={"wide": ahead(e, other)}, device_id_type=MESH)
         copy.start()
         own_copies.append(copy)
+
+    lane_in = lax.broadcasted_iota(jnp.int32, (LANES, LANES), 0)
+    lane_out = lax.broadcasted_iota(jnp.int32, (LANES, LANES), 1)
+    before = (lane_in < lane_out).astype(F32).astype(BF16)
+    ones = jnp.ones((LANES, LANES), BF16)
+    slot_ids = lax.broadcasted_iota(jnp.int32, (all_slots, LANES), 0).astype(F32)
+    columns = (lax.broadcasted_iota(jnp.int32, (half_rows, LANES), 0) * LANES
+               + lax.broadcasted_iota(jnp.int32, (half_rows, LANES), 1))
+
+    def marks(owner, block):
+        return owner != k * (width * wide_count) + block * width + half + columns
+
+    def index(e, other):
+        place = place_buf[other] if e > 0 else jnp.zeros((all_slots, LANES), F32)
+        chip = lax.rem(g - e + chips, chips)
+        block = chip * 2 + (1 - c if other else c)
+        owner = own_ref[half_rows:, :] if (e, other) == (0, 0) else owners[2 * e + other, half_rows:, :]
+        repeated = marks(owner, block)
+        flags = repeated.astype(F32).astype(BF16)
+        ranks = jnp.dot(flags, before, preferred_element_type=F32)
+        counts = jnp.dot(flags, ones, preferred_element_type=F32)
+        target = (owner - k * (width * wide_count) + 1).astype(F32)
+        base = jnp.zeros((1, LANES), F32) + (chip * slots).astype(F32)
+        for r in range(half_rows):
+            slot = jnp.where(repeated[r : r + 1, :], ranks[r : r + 1, :] + base, -1.0)
+            base = base + counts[r : r + 1, :]
+            chosen = slot_ids == slot
+            place = place + jnp.where(chosen, target[r : r + 1, :], 0.0)
+            if other == 0:
+                hot[chip, :, r * LANES : (r + 1) * LANES] = chosen.astype(F32).astype(BF16)
+        place_buf[other] = place
+
+    index(0, 0)
 
     for d in range(1, col_count):
         source = lax.rem(k - d + col_count, col_count)
@@ -100,11 +134,19 @@
         sib_copies[(e, q)].wait_recv()
         mine[e, q] += sib_in[e, q]
         if e > 0:
-            copy = pltpu.make_async_remote_copy(
-                mine.at[e, q], far_in.at[e - 1, q], far_send.at[e - 1, q], far_recv.at[e - 1, q],
-                device_id={"wide": ahead(e, 0)}, device_id_type=MESH)
-            copy.start()
-            sent.append((e, q, copy))
+            value = mine[e, q]
+            top = jnp.maximum(jnp.max(jnp.abs(value), axis=0, keepdims=True), 1e-30)
+            far_out[e - 1, q] = jnp.round(value * (LEVELS / top)).astype(jnp.int32).astype(jnp.int16)
+            top_out[e - 1, q] = top * (1.0 / LEVELS)
+            copies = []
+            for source, target, send, recv in (
+                (far_out, far_in, far_send, far_recv), (top_out, top_in, top_send, top_recv)):
+                copy = pltpu.make_async_remote_copy(
+                    source.at[e - 1, q], target.at[e - 1, q], send.at[e - 1, q], recv.at[e - 1, q],
+                    device_id={"wide": ahead(e, 0)}, device_id_type=MESH)
+                copy.start()
+                copies.append(copy)
+            sent.append((e, q, copies))
 
     sib_copies = {}
     for n, (e, q) in enumerate(steps):
@@ -121,37 +163,13 @@
 
     for copy in own_copies:
         copy.wait_recv()
-    lane_in = lax.broadcasted_iota(jnp.int32, (LANES, LANES), 0)
-    lane_out = lax.broadcasted_iota(jnp.int32, (LANES, LANES), 1)
-    before = (lane_in < lane_out).astype(F32).astype(BF16)
-    ones = jnp.ones((LANES, LANES), BF16)
-    slot_ids = lax.broadcasted_iota(jnp.int32, (all_slots, LANES), 0).astype(F32)
-    columns = (lax.broadcasted_iota(jnp.int32, (half_rows, LANES), 0) * LANES
-               + lax.broadcasted_iota(jnp.int32, (half_rows, LANES), 1))
-
-    def marks(owner, block):
-        return owner != k * (width * wide_count) + block * width + half + columns
-
+    for e, other in pairs:
+        index(e, other)
     for other in (0, 1):
-        place = jnp.zeros((all_slots, LANES), F32)
-        for e in range(chips):
-            chip = lax.rem(g - e + chips, chips)
-            block = chip * 2 + (1 - c if other else c)
-            owner = own_ref[half_rows:, :] if (e, other) == (0, 0) else owners[2 * e + other, half_rows:, :]
-            repeated = marks(owner, block)
-            flags = repeated.astype(F32).astype(BF16)
-            ranks = jnp.dot(flags, before, preferred_element_type=F32)
-            counts = jnp.dot(flags, ones, preferred_element_type=F32)
-            target = (owner - k * (width * wide_count) + 1).astype(F32)
-            base = jnp.zeros((1, LANES), F32) + (chip * slots).astype(F32)
-            for r in range(half_rows):
-                slot = jnp.where(repeated[r : r + 1, :], ranks[r : r + 1, :] + base, -1.0)
-                base = base + counts[r : r + 1, :]
-                chosen = slot_ids == slot
-                place = place + jnp.where(chosen, target[r : r + 1, :], 0.0)
-                if other == 0:
-                    hot[chip, :, r * LANES : (r + 1) * LANES] = chosen.astype(F32).astype(BF16)
-        place_buf[other] = jnp.sum(place, axis=1, keepdims=True) - 1.0
+        place = jnp.sum(place_buf[other], axis=1, keepdims=True) - 1.0
+        for q in range(chunks // 2):
+            ids = lax.broadcasted_iota(jnp.int32, (all_slots, chunk), 1) + (w * width + q * chunk)
+            lands[other, :, q * chunk : (q + 1) * chunk] = (ids.astype(F32) == place).astype(F32).astype(BF16)
 
     nt = (((1,), (1,)), ((), ()))
     picked = jnp.zeros((2 * sensors, all_slots), F32)
@@ -180,18 +198,17 @@
         sums[other] = value if sums[other] is None else sums[other] + value
     sums = [split(value) for value in sums]
     for q in range(chunks // 2):
-        mine_at = (lax.broadcasted_iota(jnp.int32, (all_slots, chunk), 1) + (w * width + q * chunk)).astype(F32)
         for other in (0, 1):
-            lands = (mine_at == place_buf[other]).astype(F32).astype(BF16)
-            added = jnp.dot(sums[other], lands, preferred_element_type=F32)
+            added = jnp.dot(sums[other], lands[other, :, q * chunk : (q + 1) * chunk], preferred_element_type=F32)
             mine[0, q] += added[:sensors] + added[sensors:]
 
     for q in range(chunks):
         value = mine[0, q]
         for e, at, copy in sent:
             if at == q:
-                copy.wait_recv()
-                value = value + far_in[e - 1, q]
+                for part in copy:
+                    part.wait_recv()
+                value = value + far_in[e - 1, q].astype(jnp.int32).astype(F32) * top_in[e - 1, q]
         if q >= chunks // 2:
             first = (q - chunks // 2) * chunk // LANES
             parts = []
@@ -201,7 +218,7 @@
             value = jnp.concatenate(parts, axis=1)
         out_ref[:, q * chunk : (q + 1) * chunk] = value
 
-    for copy in adj_copies + own_copies + dup_copies + list(sib_copies.values()) + [s[2] for s in sent]:
+    for copy in adj_copies + own_copies + dup_copies + list(sib_copies.values()) + [part for s in sent for part in s[2]]:
         copy.wait_send()
 
 
@@ -232,15 +249,20 @@
             pltpu.VMEM(pieces, F32),
             pltpu.VMEM(pieces, F32),
             pltpu.VMEM(pieces, F32),
-            pltpu.VMEM((chips - 1,) + pieces[1:], F32),
+            pltpu.VMEM((chips - 1,) + pieces[1:], jnp.int16),
+            pltpu.VMEM((chips - 1,) + pieces[1:], jnp.int16),
+            pltpu.VMEM((chips - 1, chunks, 1, chunk), F32),
+            pltpu.VMEM((chips - 1, chunks, 1, chunk), F32),
             pltpu.VMEM((chips, all_slots, half), BF16),
-            pltpu.VMEM((2, all_slots, 1), F32),
+            pltpu.VMEM((2, all_slots, half), BF16),
+            pltpu.VMEM((2, all_slots, LANES), F32),
             pltpu.VMEM((sensors, all_slots), F32),
             pltpu.VMEM((wide_count, sensors, all_slots), F32),
             dma((wide_count * chunks,)),
             dma((col_count - 1,)), dma((col_count - 1,)),
             dma((wide_count,)), dma((wide_count,)),
             dma(pieces[:2]), dma(pieces[:2]),
+            dma((chips - 1, chunks)), dma((chips - 1, chunks)),
             dma((chips - 1, chunks)), dma((chips - 1, chunks)),
             dma((wide_count,)), dma((wide_count,)),
         ],

time: 35.6 us -> 27.7 us (0.78)
  Pallas kernels: 33.3 us -> 25.4 us
    pallas_call x1, Pallas kernels: 33.3 us -> 25.4 us  [local(): pl.pallas_call(functools.partial(kernel, wide_count, col_count, chunks),...]
where the time goes in v2:
time: 27.7 us; the launch traced here: 27.4 us
  Pallas kernels  25.4 us (92%)
  local copies, waits for them, and re-layouts  2.06 us (7%)
    pallas_call x1, Pallas kernels, local(): pl.pallas_call(functools.partial(kernel, wide_count, col_count, chunks),...  25.4 us
    unnamed x1, local copies, waits for them, and re-layouts  2.06 us

profile of v2, /device:TPU:0, one launch (start us, length us, event | category | flops | bytes accessed | tf_op | source)
XLA Modules:
  0.0 27.4 jit_solution(13776234857135582227)
XLA Ops:
  0.0 25.4 %shard_map.37 = f32[32,6144]{1,0:T(8,128)} custom-call(bf16[32,48]{1,0:T(8,128)(2,1)} %adj_ref.1, bf16[384,24576]{1,0:T(8,128)(2,1)} %op_ref.1, s32[48,128]{1,0:T(8,128)} %bitcast.1), custom_call_target="tpu_custom_call" | custom-call | flops 603979776 | bytes 18874368 | tf_op jit(solution)/shard_map/pallas_call | solution.py:239
  25.4 2.1 %copy.5 = f32[32,6144]{1,0:T(8,128)} copy(f32[32,6144]{1,0:T(8,128)} %shard_map.37) | data formatting | bytes 1572864

commit v3 on v2

--- a/solution.py
+++ b/solution.py
@@ -40,7 +40,8 @@
     def ahead(e, other):
         return lax.rem(g + e, chips) * 2 + (1 - c if other else c)
 
-    steps = [(e, q) for e in list(range(1, chips)) + [0] for q in range(chunks)]
+    steps = [(e, q) for e in range(1, chips) for q in range(chunks)]
+    steps += [(0, (q + chunks // 2) % chunks) for q in range(chunks)]
     loads = []
     for n, (e, q) in enumerate(steps):
         for other in (1, 0):
@@ -148,6 +149,30 @@
                 copies.append(copy)
             sent.append((e, q, copies))
 
+    def exchange():
+        for copy in own_copies:
+            copy.wait_recv()
+        for e, other in pairs:
+            index(e, other)
+        nt = (((1,), (1,)), ((), ()))
+        picked = jnp.zeros((2 * sensors, all_slots), F32)
+        for e in range(chips):
+            for q in range(chunks // 2, chunks):
+                start = (q - chunks // 2) * chunk
+                picked += lax.dot_general(
+                    split(mine[e, q]), hot[lax.rem(g + e, chips), :, start : start + chunk], nt,
+                    preferred_element_type=F32)
+        dup_out[...] = picked[:sensors] + picked[sensors:]
+        dup_copies = []
+        for e, other in pairs:
+            at = 2 * e + other
+            copy = pltpu.make_async_remote_copy(
+                dup_out, dup_in.at[at], dup_send.at[at], dup_recv.at[at],
+                device_id={"wide": ahead(e, other)}, device_id_type=MESH)
+            copy.start()
+            dup_copies.append(copy)
+        return dup_copies
+
     sib_copies = {}
     for n, (e, q) in enumerate(steps):
         sib_out[e, q] = product(2 * n)
@@ -159,35 +184,16 @@
         mine[e, q] = product(2 * n + 1)
         if n > 0:
             combine(*steps[n - 1])
+        if (e, q) == (0, 0):
+            dup_copies = exchange()
     combine(*steps[-1])
 
-    for copy in own_copies:
-        copy.wait_recv()
-    for e, other in pairs:
-        index(e, other)
     for other in (0, 1):
         place = jnp.sum(place_buf[other], axis=1, keepdims=True) - 1.0
         for q in range(chunks // 2):
             ids = lax.broadcasted_iota(jnp.int32, (all_slots, chunk), 1) + (w * width + q * chunk)
             lands[other, :, q * chunk : (q + 1) * chunk] = (ids.astype(F32) == place).astype(F32).astype(BF16)
 
-    nt = (((1,), (1,)), ((), ()))
-    picked = jnp.zeros((2 * sensors, all_slots), F32)
-    for e in range(chips):
-        for q in range(chunks // 2, chunks):
-            start = (q - chunks // 2) * chunk
-            picked += lax.dot_general(
-                split(mine[e, q]), hot[lax.rem(g + e, chips), :, start : start + chunk], nt,
-                preferred_element_type=F32)
-    dup_out[...] = picked[:sensors] + picked[sensors:]
-    dup_copies = []
-    for e, other in pairs:
-        at = 2 * e + other
-        copy = pltpu.make_async_remote_copy(
-            dup_out, dup_in.at[at], dup_send.at[at], dup_recv.at[at],
-            device_id={"wide": ahead(e, other)}, device_id_type=MESH)
-        copy.start()
-        dup_copies.append(copy)
     repeated = marks(own_ref[half_rows:, :], w)
     kept = 1.0 - repeated.astype(F32)
     for copy in dup_copies:

time: 27.7 us -> 27.7 us (level)
  no operation moved by 1% of the time
where the time goes in v3:
time: 27.7 us; the launch traced here: 27.5 us
  Pallas kernels  25.4 us (92%)
  local copies, waits for them, and re-layouts  2.06 us (7%)
    pallas_call x1, Pallas kernels, local(): pl.pallas_call(functools.partial(kernel, wide_count, col_count, chunks),...  25.4 us
    unnamed x1, local copies, waits for them, and re-layouts  2.06 us

profile of v3, /device:TPU:0, one launch (start us, length us, event | category | flops | bytes accessed | tf_op | source)
XLA Modules:
  0.0 27.5 jit_solution(524069514189996954)
XLA Ops:
  0.0 25.4 %shard_map.37 = f32[32,6144]{1,0:T(8,128)} custom-call(bf16[32,48]{1,0:T(8,128)(2,1)} %adj_ref.1, bf16[384,24576]{1,0:T(8,128)(2,1)} %op_ref.1, s32[48,128]{1,0:T(8,128)} %bitcast.1), custom_call_target="tpu_custom_call" | custom-call | flops 603979776 | bytes 18874368 | tf_op jit(solution)/shard_map/pallas_call | solution.py:245
  25.4 2.1 %copy.5 = f32[32,6144]{1,0:T(8,128)} copy(f32[32,6144]{1,0:T(8,128)} %shard_map.37) | data formatting | bytes 1572864
